TPU v7x, 256 devices: a whole 4x4x8 slice. The times are simulated.
256 devices in a mesh: tok: 32 (over z, y_lo, core), tp: 8 (over y_hi, x).
Axes of the slice: x: 4, y: 4 (y_hi: 2, y_lo: 2; y = y_hi * 2 + y_lo), z: 8, core: 2. Of those that a mesh axis runs over, the one named last changes fastest.
Arguments:
- hidden_in: bfloat16 [8192, 4096], P('tok', 'tp'), may hold values from -6 to 6
- norm_gain: float32 [4096], replicated, may hold values from 0.5 to 9, as said below
- w_query: bfloat16 [4096, 4096], P(None, 'tp'), may hold values from -0.09375 to 0.09375
- w_key: bfloat16 [4096, 1024], P(None, 'tp'), may hold values from -0.09375 to 0.09375
- w_value: bfloat16 [4096, 1024], P(None, 'tp'), may hold values from -0.09375 to 0.09375
- w_out: bfloat16 [4096, 4096], P('tp'), may hold values from -0.5 to 0.5
- doc_ids: int32 [8192], replicated, may hold values from 0 to 3, never falling along the last dimension, each value on 1 to 6144 neighbouring positions
Outputs:
- hidden_out: bfloat16 [8192, 4096], P('tok', 'tp')
- joint_cov: float32 [2, 4096, 2, 4096], P(None, 'tok', None, 'tp')
Inputs may be any that keep to these rules, and one draw needn't show every extreme that they name: `norm_gain`: each channel's gain is positive. `doc_ids`: document numbers never fall along the tokens; a document holds 1 to 6144 tokens.
All inputs are finite; a program needn't handle non-finite values.
Results may differ from a plain program's by a relative error of at most 0.013.
The roundings to bfloat16 on the way count: a program that leaves them out, or rounds other values in their place, can miss the bound.
Values may be sent and summed in bfloat16 or wider, within the bound.
No kernel may reach another device: no remote copies, remote signals or barrier semaphores. Data moves between devices by JAX's collectives and lax.ppermute only.
A program may use at most 128 MiB of HBM per device.

v0:
```python
import jax
import jax.numpy as jnp
from jax import lax
from jax.sharding import PartitionSpec as P

HS = 128
epsilon = 1e-05
rope_base = 500000.0


def laid_out(blocks, dim):
    blocks = jnp.moveaxis(blocks, 0, dim)
    dims = blocks.shape
    return blocks.reshape(*dims[:dim], dims[dim] * dims[dim + 1], *dims[dim + 2 :])


def copy_for_each(x, axis):
    copies = jnp.broadcast_to(x, (lax.axis_size(axis), *x.shape))
    return lax.all_to_all(copies, axis, split_axis=0, concat_axis=0, tiled=True)


def collect(x, axis, dim):
    return laid_out(copy_for_each(x, axis), dim)


def in_one_piece(arrays, axis, dim, along):
    ends, at = ([], 0)
    for a in arrays[:-1]:
        at += a.shape[along]
        ends.append(at)
    both = jnp.concatenate(arrays, axis=along)
    return tuple(jnp.split(lax.all_gather(both, axis, axis=dim, tiled=True), ends, axis=along))


def rotate(vectors, positions):
    half_dim = vectors.shape[-1] // 2
    inv_freq = rope_base ** (-(jnp.arange(half_dim, dtype=jnp.float32) * 2.0) / vectors.shape[-1])
    angles = positions.astype(jnp.float32)[:, None] * inv_freq[None, :]
    cosine = jnp.cos(angles)[:, None, :]
    sine_part = jnp.sin(angles)[:, None, :]
    first_half = vectors[..., :half_dim]
    second_half = vectors[..., half_dim:]
    return jnp.concatenate(
        [
            first_half * cosine - second_half * sine_part,
            second_half * cosine + first_half * sine_part,
        ],
        axis=-1,
    )


def on_device(hidden_in, norm_gain, w_query, w_key, w_value, w_out, doc_ids):
    tok_rows = hidden_in.shape[0]
    col_width = hidden_in.shape[1]
    tok_count = lax.axis_size("tok")
    tok_index = lax.axis_index("tok")
    tp_index = lax.axis_index("tp")
    all_rows = tok_rows * tok_count
    full_in = collect(hidden_in, "tp", 1)
    model_width = full_in.shape[1]
    row_width = model_width // tok_count
    widened = full_in.astype(jnp.float32)
    factor = lax.rsqrt(jnp.mean(widened * widened, axis=1, keepdims=True) + epsilon)
    normed = (widened * factor * norm_gain[None, :]).astype(jnp.bfloat16)
    kv_heads = w_key.shape[1] // HS
    groups = w_query.shape[1] // w_key.shape[1]
    first_row = tok_index * tok_rows
    positions = first_row + jnp.arange(tok_rows, dtype=jnp.int32)
    key_local = rotate(
        jnp.dot(normed, w_key, preferred_element_type=jnp.float32).reshape(tok_rows, kv_heads, HS),
        positions % all_rows,
    )
    key_local = key_local.astype(jnp.bfloat16).reshape(tok_rows, kv_heads * HS)
    value_local = jnp.dot(normed, w_value, preferred_element_type=jnp.float32).astype(jnp.bfloat16)
    key_rows, value_rows = in_one_piece((key_local, value_local), "tok", 0, 1)
    queries = rotate(
        jnp.dot(normed, w_query, preferred_element_type=jnp.float32).reshape(
            tok_rows, kv_heads * groups, HS
        ),
        positions % all_rows,
    )
    queries = queries.astype(jnp.bfloat16).reshape(tok_rows, kv_heads, groups, HS)
    key_seq = key_rows.reshape(all_rows, kv_heads, HS)
    value_seq = value_rows.reshape(all_rows, kv_heads, HS)
    key_pos = jnp.arange(all_rows, dtype=jnp.int32)
    query_doc = lax.dynamic_slice_in_dim(doc_ids, first_row, tok_rows, 0)
    allowed = (query_doc[:, None] == doc_ids[None, :]) & (key_pos[None, :] <= positions[:, None])
    scores = jnp.einsum(
        "qhgd,khd->hgqk", queries, key_seq, preferred_element_type=jnp.float32
    ) * HS ** (-0.5)
    scores = jnp.where(allowed[None, None], scores, -jnp.inf)
    row_max = jnp.max(scores, axis=-1, keepdims=True)
    weights = jnp.exp(scores - row_max)
    weight_sum = jnp.sum(weights, axis=-1, keepdims=True)
    blended = (
        jnp.einsum(
            "hgqk,khd->hgqd",
            weights.astype(jnp.bfloat16),
            value_seq,
            preferred_element_type=jnp.float32,
        )
        / weight_sum
    )
    attended = (
        jnp.transpose(blended, (2, 0, 1, 3))
        .astype(jnp.bfloat16)
        .reshape(tok_rows, kv_heads * groups * HS)
    )
    partial_out = jnp.dot(attended, w_out, preferred_element_type=jnp.float32)
    summed = lax.psum(partial_out, "tp")
    full_out = (widened + summed).astype(jnp.bfloat16)
    hidden_out = lax.dynamic_slice_in_dim(full_out, tp_index * col_width, col_width, 1)
    joint_local = jnp.stack(
        [
            full_in.reshape(tok_rows, tok_count, row_width),
            full_out.reshape(tok_rows, tok_count, row_width),
        ],
        axis=1,
    )
    row_block = lax.all_to_all(joint_local, "tok", split_axis=2, concat_axis=0, tiled=True).reshape(
        all_rows, 2 * row_width
    )
    portion = lax.all_gather(jnp.stack([hidden_in, hidden_out], axis=1), "tok", axis=0, tiled=True)
    piece_rows = portion.shape[0]
    flat_part = portion.reshape(piece_rows, 2 * col_width)
    product = lax.dot_general(
        row_block, flat_part, (((0,), (0,)), ((), ())), preferred_element_type=jnp.float32
    )
    col_sum = jnp.sum(flat_part, axis=0, dtype=jnp.float32)
    row_mean = jnp.sum(row_block, axis=0, dtype=jnp.float32) / all_rows
    col_mean = col_sum / all_rows
    joint_cov = (product / all_rows - row_mean[:, None] * col_mean[None, :]).reshape(
        2, row_width, 2, col_width
    )
    return (hidden_out, joint_cov)


def solution(mesh):
    return jax.shard_map(
        on_device,
        mesh=mesh,
        in_specs=(
            P("tok", "tp"),
            P(),
            P(None, "tp"),
            P(None, "tp"),
            P(None, "tp"),
            P("tp", None),
            P(),
        ),
        out_specs=(P("tok", "tp"), P(None, "tok", None, "tp")),
        check_vma=False,
    )
```

profile of v0, /device:TPU:1, one launch (start us, length us, event | category | flops | bytes accessed | tf_op | source)
XLA Modules:
  0.0 543.1 jit_solution(12067020020564749845)
XLA Ops:
  7.2 1.2 copy.29
  8.4 1.5 broadcast_in_dim.10
  9.8 7.5 %all-to-all-start = ((bf16[8,256,512]{1,2,0:T(8,128)(2,1)}), bf16[8,256,512]{1,2,0:T(8,128)(2,1)S(1)}, u32[]{:S(2)}, u32[]{:S(2)}) async-start(bf16[8,256,512]{1,2,0:T(8,128)(2,1)} %broadcast_in_dim.10), calls=%async_computation | async-start | bytes 4194304 | tf_op jit(solution)/shard_map/all_to_all | solution.py:19
  17.3 0.0 all-gather.3.cloned.1.call-start
  17.4 28.5 %all-to-all-done = bf16[8,256,512]{1,2,0:T(8,128)(2,1)S(1)} async-done(((bf16[8,256,512]{1,2,0:T(8,128)(2,1)}), bf16[8,256,512]{1,2,0:T(8,128)(2,1)S(1)}, u32[]{:S(2)}, u32[]{:S(2)}) %all-to-all-start) | async-done | bytes 2097184 | tf_op jit(solution)/shard_map/all_to_all | solution.py:19
  45.9 0.6 multiply_reduce_fusion
  46.5 2.3 bitcast_convert_fusion
  48.8 5.7 %copy.44 = f32[256,4096]{1,0:T(8,128)} copy(f32[256,4096]{0,1:T(8,128)} %bitcast.92) | data formatting | bytes 8388608 | tf_op jit(solution)/shard_map/convert_element_type | solution.py:62
  54.4 2.9 multiply_convert_fusion.1
  57.3 0.8 convolution_convert_fusion
  58.2 0.8 convolution_bitcast_fusion
  59.0 0.3 fusion.28
  59.3 0.7 pad_maximum_fusion.2
  60.0 0.0 all-gather.3.cloned.1.call-update
  60.0 0.2 all-reduce.2.cloned.1.call-start
  60.3 6.4 %copy.47 = bf16[512,4096]{1,0:T(8,128)(2,1)} copy(bf16[512,4096]{0,1:T(8,128)(2,1)} %bitcast.95) | data formatting | bytes 8388608 | tf_op jit(solution)/shard_map/dot_general | solution.py:77
  66.7 0.1 dynamic_slice.6
  66.8 0.3 multiply_cosine_fusion
  67.1 4.7 fusion.7
  71.8 0.7 multiply_convert_fusion
  72.5 1.3 fusion.34
  73.8 0.1 subtract_convert_fusion
  73.8 61.0 %all-gather.3.cloned.1.call-done = bf16[8192,256]{0,1:T(8,128)(2,1)} async-done(((bf16[256,256]{0,1:T(8,128)(2,1)}), bf16[8192,256]{0,1:T(8,128)(2,1)}) %all-gather.3.cloned.1.call-update) | async-done | bytes 4194320 | tf_op jit(solution)/shard_map/all_gather | solution.py:32
  134.9 15.3 %fusion.2 = (f32[4,256]{1,0:T(4,128)S(1)}, f32[8192,256,4]{1,0,2:T(8,128)}) fusion(pred[256,8192]{0,1:T(8,128)(4,1)} %fusion.7, bf16[256,4,64]{0,2,1:T(8,128)(2,1)S(1)} %get-tuple-element.3, bf16[256,4,64]{0,2,1:T(8,128)(2,1)S(1)} %get-tuple-element.2, bf16[8192,256]{0,1:T(8,128)(2,1)} %all-gather.3.cloned.1.call-done), kind=kOutput, calls=%fused_computation.5 | convolution fusion | flops 2173172736 | bytes 38014976 | tf_op jit(solution)/shard_map/qhgd,khd->hgqk/dot_general | solution.py:88
  150.2 14.5 %fusion = f32[4,256]{1,0:T(4,128)S(1)} fusion(f32[8192,256,4]{1,0,2:T(8,128)} %get-tuple-element.9, f32[4,256]{1,0:T(4,128)S(1)} %get-tuple-element.8, pred[256,8192]{0,1:T(8,128)(4,1)S(1)} %copy-done.3), kind=kLoop, calls=%fused_computation.3 | loop fusion | flops 33553408 | bytes 35659776 | tf_op jit(solution)/shard_map/reduce_sum | solution.py:94
  164.7 15.5 %fusion.13 = bf16[4,256,128]{1,2,0:T(8,128)(2,1)S(1)} fusion(f32[8192,256,4]{1,0,2:T(8,128)} %get-tuple-element.9, f32[4,256]{1,0:T(4,128)S(1)} %get-tuple-element.8, pred[256,8192]{0,1:T(8,128)(4,1)} %fusion.7, bf16[8192,256]{0,1:T(8,128)(2,1)} %all-gather.3.cloned.1.call-done, f32[4,256]{1,0:T(4,128)S(1)} %fusion), kind=kOutput, calls=%fused_computation.26 | convolution fusion | flops 2181300224 | bytes 38019072 | tf_op jit(solution)/shard_map/hgqk,khd->hgqd/dot_general | solution.py:96
  180.2 5.5 %fusion.35 = f32[256,4096]{1,0:T(8,128)} fusion(bf16[256,512]{0,1:T(8,128)(2,1)S(1)} %bitcast.100, bf16[512,4096]{1,0:T(8,128)(2,1)} %param.12), kind=kOutput, calls=%fused_computation.63 | convolution fusion | flops 1073741824 | bytes 8650752 | tf_op jit(solution)/shard_map/dot_general | solution.py:109
  185.6 0.0 all-reduce.2.cloned.1.call-update
  185.6 0.0 all-gather.5.cloned.1.call-start
  185.7 113.2 %all-reduce.2.cloned.1.call-done = f32[256,4096]{1,0:T(8,128)} async-done(((f32[256,4096]{1,0:T(8,128)}), f32[256,4096]{1,0:T(8,128)}) %all-reduce.2.cloned.1.call-update) | async-done | bytes 4194320 | tf_op jit(solution)/shard_map/psum | solution.py:110
  298.9 4.0 add_convert_fusion
  302.9 1.4 copy-done.2
  304.3 0.8 pad_maximum_fusion.1
  305.1 0.0 all-gather.5.cloned.1.call-update
  305.1 4.1 copy.48
  309.2 2.0 pad_maximum_fusion
  311.2 2.3 copy.37
  313.5 7.9 %all-to-all-start.1 = ((bf16[256,2,32,128]{0,3,1,2:T(8,128)(2,1)}), bf16[256,2,32,128]{0,3,1,2:T(8,128)(2,1)}, u32[]{:S(2)}, u32[]{:S(2)}) async-start(bf16[256,2,32,128]{0,3,1,2:T(8,128)(2,1)} %copy.37), calls=%async_computation.1 | async-start | bytes 8388608 | tf_op jit(solution)/shard_map/all_to_all | solution.py:120
  321.4 1.7 constant_dynamic-slice_fusion
  323.1 139.7 %all-to-all-done.1 = bf16[256,2,32,128]{0,3,1,2:T(8,128)(2,1)} async-done(((bf16[256,2,32,128]{0,3,1,2:T(8,128)(2,1)}), bf16[256,2,32,128]{0,3,1,2:T(8,128)(2,1)}, u32[]{:S(2)}, u32[]{:S(2)}) %all-to-all-start.1) | async-done | bytes 4194336 | tf_op jit(solution)/shard_map/all_to_all | solution.py:120
  462.8 4.6 copy.38
  467.4 6.4 %copy.49 = bf16[32,8,32,256]{3,1,2,0:T(8,128)(2,1)} copy(bf16[32,8,32,256]{3,2,1,0:T(8,128)(2,1)S(1)} %bitcast.93) | data formatting | bytes 8388608
  473.8 2.9 convert_reduce_fusion.1
  476.7 17.3 %all-gather.5.cloned.1.call-done = bf16[8192,2,512]{2,0,1:T(8,128)(2,1)} async-done(((bf16[256,2,512]{2,0,1:T(8,128)(2,1)}), bf16[8192,2,512]{2,0,1:T(8,128)(2,1)}) %all-gather.5.cloned.1.call-update) | async-done | bytes 16777232 | tf_op jit(solution)/shard_map/all_gather | solution.py:123
  494.0 10.3 %convert_reduce_fusion = f32[2,512]{1,0:T(2,128)S(1)} fusion(bf16[8192,2,512]{2,0,1:T(8,128)(2,1)} %all-gather.5.cloned.1.call-done), kind=kLoop, calls=%fused_computation.1 | loop fusion | flops 16776192 | bytes 16781312 | tf_op jit(solution)/shard_map/reduce_sum | solution.py:129
  504.4 20.9 %copy.39 = bf16[8192,2,512]{0,2,1:T(8,128)(2,1)} copy(bf16[8192,2,512]{2,0,1:T(8,128)(2,1)} %all-gather.5.cloned.1.call-done) | data formatting | bytes 33554432 | tf_op jit(solution)/shard_map/all_gather | solution.py:123
  525.3 9.4 %fusion.9 = f32[256,1024]{1,0:T(8,128)S(1)} fusion(bf16[8192,256]{0,1:T(8,128)(2,1)} %bitcast.97, bf16[8192,1024]{0,1:T(8,128)(2,1)} %bitcast.91, f32[1024]{0:T(1024)S(1)} %bitcast.101, f32[256]{0:T(256)S(1)} %multiply_bitcast_fusion.1), kind=kOutput, calls=%fused_computation.22 | convolution fusion | flops 4295753728 | bytes 22025216 | tf_op jit(solution)/shard_map/dot_general | solution.py:126
  534.7 1.9 reshape.283
  (26 shorter events, 0.1 us)
Async XLA Ops:
  7.2 50.1 %copy-start = (bf16[4096,128]{1,0:T(8,128)(2,1)S(1)}, bf16[4096,128]{1,0:T(8,128)(2,1)}, u32[]{:S(2)}) copy-start(bf16[4096,128]{1,0:T(8,128)(2,1)} %param.11) | copy-start | bytes 3145732
  9.8 36.0 %all-to-all-start = ((bf16[8,256,512]{1,2,0:T(8,128)(2,1)}), bf16[8,256,512]{1,2,0:T(8,128)(2,1)S(1)}, u32[]{:S(2)}, u32[]{:S(2)}) async-start(bf16[8,256,512]{1,2,0:T(8,128)(2,1)} %broadcast_in_dim.10), calls=%async_computation | async-start | bytes 4194304 | tf_op jit(solution)/shard_map/all_to_all | solution.py:19
  17.3 117.6 %all-gather.3.cloned.1.call-start = ((), (), s32[]{:S(2)}) async-start(), calls=%async_computation.2 | async-start | bytes 4325376 | tf_op jit(solution)/shard_map/all_gather | solution.py:32
  48.8 5.7 %copy-start.7 = (f32[4096]{0:T(1024)S(1)}, f32[4096]{0:T(1024)}, u32[]{:S(2)}) copy-start(f32[4096]{0:T(1024)} %param.8) | copy-start | bytes 49156
  54.4 3.7 copy-start.5
  60.0 238.9 %all-reduce.2.cloned.1.call-start = ((), (), s32[]{:S(2)}) async-start(), calls=%async_computation.3 | async-start | bytes 8388608 | tf_op jit(solution)/shard_map/psum | solution.py:110
  60.2 6.5 %copy-start.8 = (s32[8192]{0:T(1024)S(1)}, s32[8192]{0:T(1024)}, u32[]{:S(2)}) copy-start(s32[8192]{0:T(1024)} %param.13) | copy-start | bytes 98308
  66.7 5.8 %copy-start.4 = (bf16[512,4096]{1,0:T(8,128)(2,1)S(1)}, bf16[512,4096]{1,0:T(8,128)(2,1)}, u32[]{:S(2)}) copy-start(bf16[512,4096]{1,0:T(8,128)(2,1)} %copy.47) | copy-start | bytes 12582916
  134.9 15.3 %copy-start.3 = (pred[256,8192]{0,1:T(8,128)(4,1)S(1)}, pred[256,8192]{0,1:T(8,128)(4,1)}, u32[]{:S(2)}) copy-start(pred[256,8192]{0,1:T(8,128)(4,1)} %fusion.7) | copy-start | bytes 6291460
  185.6 308.4 %all-gather.5.cloned.1.call-start = ((), (), s32[]{:S(2)}) async-start(), calls=%async_computation.4 | async-start | bytes 17301504 | tf_op jit(solution)/shard_map/all_gather | solution.py:123
  185.7 118.6 %copy-start.6 = (bf16[256,512]{1,0:T(8,128)(2,1)S(1)}, bf16[256,512]{1,0:T(8,128)(2,1)}, u32[]{:S(2)}) copy-start(bf16[256,512]{1,0:T(8,128)(2,1)} %param.7) | copy-start | bytes 786436
  302.9 1.4 copy-start.2
  313.5 149.3 %all-to-all-start.1 = ((bf16[256,2,32,128]{0,3,1,2:T(8,128)(2,1)}), bf16[256,2,32,128]{0,3,1,2:T(8,128)(2,1)}, u32[]{:S(2)}, u32[]{:S(2)}) async-start(bf16[256,2,32,128]{0,3,1,2:T(8,128)(2,1)} %copy.37), calls=%async_computation.1 | async-start | bytes 8388608 | tf_op jit(solution)/shard_map/all_to_all | solution.py:120
  525.3 11.3 %copy-start.1 = (bf16[4096,128]{1,0:T(8,128)(2,1)S(1)}, bf16[4096,128]{1,0:T(8,128)(2,1)}, u32[]{:S(2)}) copy-start(bf16[4096,128]{1,0:T(8,128)(2,1)} %param.11) | copy-start | bytes 3145732
Sparse Core Ops, SparseCore 0:
  60.1 74.7 all-gather.2
  185.8 113.0 all-reduce.1
  305.3 188.7 all-gather.4
where the time goes:
time: 544 us; the launch traced here: 543 us
  waiting for transfers between devices  360 us (66%)
  local copies, waits for them, and re-layouts  58 us (11%)
  matrix products  48.6 us (9%)
  other arithmetic  47.1 us (9%)
  starting transfers between devices  15.7 us (3%)
  between operations  14 us (3%)
    all_to_all x1, waiting for transfers between devices, on_device(): lax.all_to_all(joint_local, 'tok', split_axis=2, concat_axis=0, tiled=True)  140 us
    psum x1, waiting for transfers between devices, on_device(): summed = lax.psum(partial_out, 'tp')  113 us
    all_gather x1, waiting for transfers between devices, in_one_piece(): lax.all_gather(both, axis, axis=dim, tiled=True)  61 us
    all_to_all x1, waiting for transfers between devices, copy_for_each(): return lax.all_to_all(copies, axis, split_axis=0, concat_axis=0, tiled=True)  28.5 us
    all_gather x1, local copies, waits for them, and re-layouts, on_device(): lax.all_gather(jnp.stack([hidden_in, hidden_out], axis=1), 'tok', axis=0,...  20.9 us
    all_gather x1, waiting for transfers between devices, on_device(): lax.all_gather(jnp.stack([hidden_in, hidden_out], axis=1), 'tok', axis=0,...  17.3 us
    dot_general x1, matrix products, on_device(): jnp.einsum('hgqk,khd->hgqd', weights.astype(jnp.bfloat16), value_seq, pre...  15.5 us
    dot_general x1, matrix products, on_device(): jnp.einsum('qhgd,khd->hgqk', queries, key_seq, preferred_element_type=jnp...  15.3 us
  transfers between devices with their start and end apart: 5, of which 5 were waited for; matrix products, arithmetic and copies ran while one was open for 7% of the time, Pallas kernels for 0%

commit v1 on v0

--- a/solution.py
+++ b/solution.py
@@ -1,3 +1,4 @@
+import functools
 import jax
 import jax.numpy as jnp
 from jax import lax
@@ -6,6 +7,18 @@
 HS = 128
 epsilon = 1e-05
 rope_base = 500000.0
+
+
+def _apply_weights(q_in, k_dim, axis_k):
+    return jnp.concatenate(
+        lax.all_to_all(
+            jnp.stack(jnp.split(q_in, lax.psum(1, "tok"), axis=k_dim), axis=0), "tok", 0, 0
+        ),
+        axis=axis_k,
+    )
+
+
+extend_leaves_up = functools.partial(_apply_weights, k_dim=2, axis_k=0)
 
 
 def laid_out(blocks, dim):
@@ -117,9 +130,7 @@
         ],
         axis=1,
     )
-    row_block = lax.all_to_all(joint_local, "tok", split_axis=2, concat_axis=0, tiled=True).reshape(
-        all_rows, 2 * row_width
-    )
+    row_block = extend_leaves_up(joint_local).reshape(all_rows, 2 * row_width)
     portion = lax.all_gather(jnp.stack([hidden_in, hidden_out], axis=1), "tok", axis=0, tiled=True)
     piece_rows = portion.shape[0]
     flat_part = portion.reshape(piece_rows, 2 * col_width)

time: 544 us -> 546 us (level)
  other arithmetic: 47.1 us -> 67.3 us
  waiting for transfers between devices: 360 us -> 343 us
    unnamed x1 -> x32, other arithmetic: 0.01 us -> 21.6 us
    all_gather x1, waiting for transfers between devices: 17.3 us -> 0.02 us  [on_device(): lax.all_gather(jnp.stack([hidden_in, hidden_out], axis=1), 'tok', axis=0,...]
  transfers between devices with their start and end apart: 5 -> 5, of which waited for: 5 -> 4; matrix products, arithmetic and copies ran while one was open for 7% -> 10% of each run, Pallas kernels for 0% -> 0%
where the time goes in v1:
time: 546 us; the launch traced here: 544 us
  waiting for transfers between devices  343 us (63%)
  other arithmetic  67.3 us (12%)
  local copies, waits for them, and re-layouts  56.3 us (10%)
  matrix products  48.6 us (9%)
  starting transfers between devices  15.7 us (3%)
  between operations  14 us (3%)
    all_to_all x1, waiting for transfers between devices, _apply_weights(): lax.all_to_all(jnp.stack(jnp.split(q_in, lax.psum(1, 'tok'), axis=k_dim),...  140 us
    psum x1, waiting for transfers between devices, on_device(): summed = lax.psum(partial_out, 'tp')  113 us
    all_gather x1, waiting for transfers between devices, in_one_piece(): lax.all_gather(both, axis, axis=dim, tiled=True)  61.1 us
    all_to_all x1, waiting for transfers between devices, copy_for_each(): return lax.all_to_all(copies, axis, split_axis=0, concat_axis=0, tiled=True)  28.5 us
    unnamed x32, other arithmetic  21.6 us
    all_gather x1, local copies, waits for them, and re-layouts, on_device(): lax.all_gather(jnp.stack([hidden_in, hidden_out], axis=1), 'tok', axis=0,...  21.4 us
    dot_general x1, matrix products, on_device(): jnp.einsum('hgqk,khd->hgqd', weights.astype(jnp.bfloat16), value_seq, pre...  15.5 us
    dot_general x1, matrix products, on_device(): jnp.einsum('qhgd,khd->hgqk', queries, key_seq, preferred_element_type=jnp...  15.3 us
  transfers between devices with their start and end apart: 5, of which 4 were waited for; matrix products, arithmetic and copies ran while one was open for 10% of the time, Pallas kernels for 0%

profile of v1, /device:TPU:1, one launch (start us, length us, event | category | flops | bytes accessed | tf_op | source)
XLA Modules:
  0.0 544.3 jit_solution(2448292159534658929)
XLA Ops:
  7.2 1.2 copy.81
  8.4 1.5 broadcast_in_dim.10
  9.8 7.5 %all-to-all-start = ((bf16[8,256,512]{1,2,0:T(8,128)(2,1)}), bf16[8,256,512]{1,2,0:T(8,128)(2,1)S(1)}, u32[]{:S(2)}, u32[]{:S(2)}) async-start(bf16[8,256,512]{1,2,0:T(8,128)(2,1)} %broadcast_in_dim.10), calls=%async_computation | async-start | bytes 4194304 | tf_op jit(solution)/shard_map/all_to_all | solution.py:32
  17.4 28.5 %all-to-all-done = bf16[8,256,512]{1,2,0:T(8,128)(2,1)S(1)} async-done(((bf16[8,256,512]{1,2,0:T(8,128)(2,1)}), bf16[8,256,512]{1,2,0:T(8,128)(2,1)S(1)}, u32[]{:S(2)}, u32[]{:S(2)}) %all-to-all-start) | async-done | bytes 2097184 | tf_op jit(solution)/shard_map/all_to_all | solution.py:32
  46.5 2.3 bitcast_convert_fusion
  48.8 5.7 %copy.127 = f32[256,4096]{1,0:T(8,128)} copy(f32[256,4096]{0,1:T(8,128)} %bitcast.277) | data formatting | bytes 8388608 | tf_op jit(solution)/shard_map/convert_element_type | solution.py:75
  54.5 2.9 multiply_convert_fusion.1
  57.3 0.8 convolution_convert_fusion
  58.2 0.8 convolution_bitcast_fusion
  59.3 0.7 pad_maximum_fusion.2
  60.3 6.4 %copy.130 = bf16[512,4096]{1,0:T(8,128)(2,1)} copy(bf16[512,4096]{0,1:T(8,128)(2,1)} %bitcast.279) | data formatting | bytes 8388608 | tf_op jit(solution)/shard_map/dot_general | solution.py:90
  67.1 4.7 fusion.7
  71.8 0.7 multiply_convert_fusion
  72.5 1.2 fusion.67
  73.8 61.1 %all-gather.3.cloned.1.call-done = bf16[8192,256]{0,1:T(8,128)(2,1)} async-done(((bf16[256,256]{0,1:T(8,128)(2,1)}), bf16[8192,256]{0,1:T(8,128)(2,1)}) %all-gather.3.cloned.1.call-update) | async-done | bytes 4194320 | tf_op jit(solution)/shard_map/all_gather | solution.py:45
  134.9 15.3 %fusion.2 = (f32[4,256]{1,0:T(4,128)S(1)}, f32[8192,256,4]{1,0,2:T(8,128)}) fusion(pred[256,8192]{0,1:T(8,128)(4,1)} %fusion.7, bf16[256,4,64]{0,2,1:T(8,128)(2,1)S(1)} %get-tuple-element.3, bf16[256,4,64]{0,2,1:T(8,128)(2,1)S(1)} %get-tuple-element.2, bf16[8192,256]{0,1:T(8,128)(2,1)} %all-gather.3.cloned.1.call-done), kind=kOutput, calls=%fused_computation.5 | convolution fusion | flops 2173172736 | bytes 38014976 | tf_op jit(solution)/shard_map/qhgd,khd->hgqk/dot_general | solution.py:101
  150.2 14.5 %fusion = f32[4,256]{1,0:T(4,128)S(1)} fusion(f32[8192,256,4]{1,0,2:T(8,128)} %get-tuple-element.9, f32[4,256]{1,0:T(4,128)S(1)} %get-tuple-element.8, pred[256,8192]{0,1:T(8,128)(4,1)S(1)} %copy-done.4), kind=kLoop, calls=%fused_computation.3 | loop fusion | flops 33553408 | bytes 35659776 | tf_op jit(solution)/shard_map/reduce_sum | solution.py:107
  164.7 15.5 %fusion.13 = bf16[4,256,128]{1,2,0:T(8,128)(2,1)S(1)} fusion(f32[8192,256,4]{1,0,2:T(8,128)} %get-tuple-element.9, f32[4,256]{1,0:T(4,128)S(1)} %get-tuple-element.8, pred[256,8192]{0,1:T(8,128)(4,1)} %fusion.7, bf16[8192,256]{0,1:T(8,128)(2,1)} %all-gather.3.cloned.1.call-done, f32[4,256]{1,0:T(4,128)S(1)} %fusion), kind=kOutput, calls=%fused_computation.87 | convolution fusion | flops 2181300224 | bytes 38019072 | tf_op jit(solution)/shard_map/hgqk,khd->hgqd/dot_general | solution.py:109
  180.2 5.4 %fusion.68 = f32[256,4096]{1,0:T(8,128)} fusion(bf16[256,512]{0,1:T(8,128)(2,1)S(1)} %bitcast.284, bf16[512,4096]{1,0:T(8,128)(2,1)} %param.12), kind=kOutput, calls=%fused_computation.189 | convolution fusion | flops 1073741824 | bytes 8650752 | tf_op jit(solution)/shard_map/dot_general | solution.py:122
  185.7 113.2 %all-reduce.2.cloned.1.call-done = f32[256,4096]{1,0:T(8,128)} async-done(((f32[256,4096]{1,0:T(8,128)}), f32[256,4096]{1,0:T(8,128)}) %all-reduce.2.cloned.1.call-update) | async-done | bytes 4194320 | tf_op jit(solution)/shard_map/psum | solution.py:123
  298.9 4.0 add_convert_fusion
  302.9 1.4 copy-done.3
  304.2 0.8 pad_maximum_fusion
  305.1 4.1 copy.131
  309.2 1.6 bitcast_dynamic-update-slice_fusion.29
  312.2 0.7 bitcast_dynamic-update-slice_fusion.26
  312.8 0.7 bitcast_dynamic-update-slice_fusion.25
  315.5 0.7 bitcast_dynamic-update-slice_fusion.21
  316.1 0.7 bitcast_dynamic-update-slice_fusion.20
  317.5 0.7 bitcast_dynamic-update-slice_fusion.18
  320.2 0.7 bitcast_dynamic-update-slice_fusion.14
  320.8 0.7 bitcast_dynamic-update-slice_fusion.13
  321.5 0.7 bitcast_dynamic-update-slice_fusion.12
  324.2 0.7 bitcast_dynamic-update-slice_fusion.8
  324.8 0.7 bitcast_dynamic-update-slice_fusion.7
  328.8 0.7 bitcast_dynamic-update-slice_fusion.1
  330.1 0.7 bitcast_dynamic-update-slice_fusion.30
  330.8 0.7 fusion.51
  331.5 7.9 %all-to-all-start.1 = ((bf16[32,256,2,1,128]{1,4,2,3,0:T(8,128)(2,1)}), bf16[32,256,2,1,128]{1,4,2,3,0:T(8,128)(2,1)}, u32[]{:S(2)}, u32[]{:S(2)}) async-start(bf16[32,256,2,1,128]{1,4,2,3,0:T(8,128)(2,1)} %fusion.51), calls=%async_computation.1 | async-start | bytes 8388608 | tf_op jit(solution)/shard_map/all_to_all | solution.py:14
  339.4 1.7 constant_dynamic-slice_fusion
  341.1 139.7 %all-to-all-done.1 = bf16[32,256,2,1,128]{1,4,2,3,0:T(8,128)(2,1)} async-done(((bf16[32,256,2,1,128]{1,4,2,3,0:T(8,128)(2,1)}), bf16[32,256,2,1,128]{1,4,2,3,0:T(8,128)(2,1)}, u32[]{:S(2)}, u32[]{:S(2)}) %all-to-all-start.1) | async-done | bytes 4194336 | tf_op jit(solution)/shard_map/all_to_all | solution.py:14
  480.8 4.6 copy.121
  485.5 6.4 %copy.163 = bf16[32,8,32,256]{3,1,2,0:T(8,128)(2,1)} copy(bf16[32,8,32,256]{3,2,1,0:T(8,128)(2,1)S(1)} %bitcast.278) | data formatting | bytes 8388608
  491.8 2.9 convert_reduce_fusion.1
  494.7 10.3 %convert_reduce_fusion = f32[2,512]{1,0:T(2,128)S(1)} fusion(bf16[8192,2,512]{2,0,1:T(8,128)(2,1)} %all-gather.5.cloned.1.call-done), kind=kLoop, calls=%fused_computation.1 | loop fusion | flops 16776192 | bytes 16781312 | tf_op jit(solution)/shard_map/reduce_sum | solution.py:140
  505.1 21.4 %copy.122 = bf16[8192,2,512]{0,2,1:T(8,128)(2,1)} copy(bf16[8192,2,512]{2,0,1:T(8,128)(2,1)} %all-gather.5.cloned.1.call-done) | data formatting | bytes 33554432 | tf_op jit(solution)/shard_map/all_gather | solution.py:134
  526.5 9.4 %fusion.9 = f32[256,1024]{1,0:T(8,128)S(1)} fusion(bf16[8192,256]{0,1:T(8,128)(2,1)} %bitcast.281, bf16[8192,1024]{0,1:T(8,128)(2,1)} %bitcast.276, f32[1024]{0:T(1024)S(1)} %bitcast.285, f32[256]{0:T(256)S(1)} %multiply_bitcast_fusion.1), kind=kOutput, calls=%fused_computation.83 | convolution fusion | flops 4295753728 | bytes 22025216 | tf_op jit(solution)/shard_map/dot_general | solution.py:137
  535.9 1.9 reshape.278
  (58 shorter events, 13.7 us)
Async XLA Ops:
  7.2 50.2 %copy-start = (bf16[4096,128]{1,0:T(8,128)(2,1)S(1)}, bf16[4096,128]{1,0:T(8,128)(2,1)}, u32[]{:S(2)}) copy-start(bf16[4096,128]{1,0:T(8,128)(2,1)} %param.11) | copy-start | bytes 3145732
  9.8 36.0 %all-to-all-start = ((bf16[8,256,512]{1,2,0:T(8,128)(2,1)}), bf16[8,256,512]{1,2,0:T(8,128)(2,1)S(1)}, u32[]{:S(2)}, u32[]{:S(2)}) async-start(bf16[8,256,512]{1,2,0:T(8,128)(2,1)} %broadcast_in_dim.10), calls=%async_computation | async-start | bytes 4194304 | tf_op jit(solution)/shard_map/all_to_all | solution.py:32
  17.3 117.6 %all-gather.3.cloned.1.call-start = ((), (), s32[]{:S(2)}) async-start(), calls=%async_computation.2 | async-start | bytes 4325376 | tf_op jit(solution)/shard_map/all_gather | solution.py:45
  48.8 5.7 %copy-start.8 = (f32[4096]{0:T(1024)S(1)}, f32[4096]{0:T(1024)}, u32[]{:S(2)}) copy-start(f32[4096]{0:T(1024)} %param.8) | copy-start | bytes 49156
  54.5 3.7 copy-start.6
  60.0 238.8 %all-reduce.2.cloned.1.call-start = ((), (), s32[]{:S(2)}) async-start(), calls=%async_computation.3 | async-start | bytes 8388608 | tf_op jit(solution)/shard_map/psum | solution.py:123
  60.3 6.4 %copy-start.9 = (s32[8192]{0:T(1024)S(1)}, s32[8192]{0:T(1024)}, u32[]{:S(2)}) copy-start(s32[8192]{0:T(1024)} %param.13) | copy-start | bytes 98308
  66.7 5.8 %copy-start.5 = (bf16[512,4096]{1,0:T(8,128)(2,1)S(1)}, bf16[512,4096]{1,0:T(8,128)(2,1)}, u32[]{:S(2)}) copy-start(bf16[512,4096]{1,0:T(8,128)(2,1)} %copy.130) | copy-start | bytes 12582916
  134.9 15.3 %copy-start.4 = (pred[256,8192]{0,1:T(8,128)(4,1)S(1)}, pred[256,8192]{0,1:T(8,128)(4,1)}, u32[]{:S(2)}) copy-start(pred[256,8192]{0,1:T(8,128)(4,1)} %fusion.7) | copy-start | bytes 6291460
  185.6 309.1 %all-gather.5.cloned.1.call-start = ((), (), s32[]{:S(2)}) async-start(), calls=%async_computation.4 | async-start | bytes 17301504 | tf_op jit(solution)/shard_map/all_gather | solution.py:134
  185.7 118.5 %copy-start.7 = (bf16[256,512]{1,0:T(8,128)(2,1)S(1)}, bf16[256,512]{1,0:T(8,128)(2,1)}, u32[]{:S(2)}) copy-start(bf16[256,512]{1,0:T(8,128)(2,1)} %param.7) | copy-start | bytes 786436
  302.8 1.4 copy-start.3
  309.2 1.6 copy-start.2
  331.5 149.3 %all-to-all-start.1 = ((bf16[32,256,2,1,128]{1,4,2,3,0:T(8,128)(2,1)}), bf16[32,256,2,1,128]{1,4,2,3,0:T(8,128)(2,1)}, u32[]{:S(2)}, u32[]{:S(2)}) async-start(bf16[32,256,2,1,128]{1,4,2,3,0:T(8,128)(2,1)} %fusion.51), calls=%async_computation.1 | async-start | bytes 8388608 | tf_op jit(solution)/shard_map/all_to_all | solution.py:14
  526.5 11.3 %copy-start.1 = (bf16[4096,128]{1,0:T(8,128)(2,1)S(1)}, bf16[4096,128]{1,0:T(8,128)(2,1)}, u32[]{:S(2)}) copy-start(bf16[4096,128]{1,0:T(8,128)(2,1)} %param.11) | copy-start | bytes 3145732
Sparse Core Ops, SparseCore 0:
  60.2 74.7 all-gather.2
  185.8 113.0 all-reduce.1
  305.2 188.7 all-gather.4
